TPU v7x, 32 devices: a whole 2x2x4 slice. The times are simulated.
32 devices in a mesh: layer: 4 (over x, core), angle: 8 (over z, y).
Axes of the slice: x: 2, y: 2, z: 4, core: 2. Of those that a mesh axis runs over, the one named last changes fastest.
Arguments:
- right_side: bfloat16 [8, 2048, 2, 96], P('layer', 'angle'), may hold values from -6 to 6
- inverse: bfloat16 [8, 2, 2048, 2048], P('layer', None, 'angle'), may hold values from -0.09375 to 0.09375
- coupling: bfloat16 [8, 4, 2, 2048, 2048], P('layer', None, None, 'angle'), may hold values from -0.046875 to 0.046875
- image_offset: int32 [8, 4], P('layer'), may hold values from 1 to 2
- image_count: int32 [8], P('layer'), may hold values from 2 to 4
- phase_exponent: int32 [8, 4], P('layer'), may hold values from -6 to 6
Outputs:
- solution: bfloat16 [8, 2048, 2, 96], P('layer', 'angle')
Inputs may be any that keep to these rules, and one draw needn't show every extreme that they name: Slot k of layer l couples to layer l - image_offset[l,k]; it couples to nothing when that index is below 0. Layer l uses its first image_count[l] slots.
All inputs are finite; a program needn't handle non-finite values.
Results may differ from a plain program's by a relative error of at most 0.015.
Values may be sent and summed in bfloat16 or wider, within the bound.
No kernel may reach another device: no remote copies, remote signals or barrier semaphores. Data moves between devices by JAX's collectives and lax.ppermute only.
A program may use at most 64 MiB of HBM per device.

v0:
```python
import functools
import math

import jax
import jax.numpy as jnp
from jax import lax
from jax.experimental import pallas as pl
from jax.experimental.pallas import tpu as pltpu
from jax.sharding import PartitionSpec as P

ANGLES = 16
NRHS = 6
CORES = 2
LIMIT = 24 * 2**20

VMEM = pl.BlockSpec(memory_space=pltpu.VMEM)
ANY = pl.BlockSpec(memory_space=pl.ANY)


def copies_kernel(source_ref, out_ref):
    for place in range(out_ref.shape[0]):
        out_ref[place] = source_ref[...]


def copies(array, count):
    return pl.pallas_call(
        copies_kernel,
        out_shape=jax.ShapeDtypeStruct((count,) + array.shape, array.dtype),
        in_specs=[VMEM],
        out_specs=VMEM,
        compiler_params=pltpu.CompilerParams(vmem_limit_bytes=LIMIT),
        name="copies",
    )(array)


def swap(array):
    pairs = [(i, i ^ 1) for i in range(lax.axis_size("layer"))]
    return lax.ppermute(array, "layer", pairs)


def shift(array, chip):
    peers = lax.axis_size("angle")
    first, last = chip * CORES * peers, (chip + 1) * CORES * peers
    return lax.ppermute(array, ("layer", "angle"), [(i, i + CORES * peers) for i in range(first, last)])


def gather(copied):
    return lax.all_to_all(copied, "angle", 0, 0)


def assemble(blocks_ref, full_ref, side):
    lines, width = full_ref.shape[0], blocks_ref.shape[2]
    half, whole = lines // 2, blocks_ref.shape[1] // 2
    for owner in range(blocks_ref.shape[0]):
        columns = slice(owner * width, (owner + 1) * width)
        for part in range(2):
            first = part * whole + side * half
            full_ref[part * half : (part + 1) * half, columns] = blocks_ref[owner, first : first + half]


def multiply(full, weights):
    return lax.dot_general(
        full,
        weights.reshape(-1, weights.shape[2]),
        (((1,), (1,)), ((), ())),
        preferred_element_type=jnp.float32,
    )


def complex_parts(product):
    cols, rows = product.shape[0] // 2, product.shape[1] // 2
    real = product[:cols, :rows] - product[cols:, rows:]
    imag = product[cols:, :rows] + product[:cols, rows:]
    return real, imag


def load_kernel(layer, plan_ref, own_ref, other_ref, _, out_ref, sem):
    layers = own_ref.shape[0]
    own = jnp.max(plan_ref[plan_ref.shape[0] - 1, 0]) == layer // layers
    mine = pltpu.make_async_copy(own_ref.at[layer % layers], out_ref, sem)
    given = pltpu.make_async_copy(other_ref.at[layer % layers], out_ref, sem)
    pl.when(own)(mine.start)
    pl.when(jnp.logical_not(own))(given.start)
    mine.wait()


def image_kernel(layer, kind, first, plan_ref, table_ref, own_ref, other_ref, base_ref, *refs):
    *blocks_refs, out_ref, total_ref, full_ref, weights, sems = refs
    wide, rows = total_ref.shape
    cols = wide // 2
    layers, slots = own_ref.shape[:2]
    core = jnp.max(plan_ref[plan_ref.shape[0] - 1, 0])
    own = core == layer // layers

    def copy(weight_ref, slot):
        return pltpu.make_async_copy(weight_ref.at[layer % layers, slot], weights.at[slot], sems.at[slot])

    for slot in range(slots):
        used = jnp.max(plan_ref[layer, slot]) == kind
        pl.when(used & own)(copy(own_ref, slot).start)
        pl.when(used & jnp.logical_not(own))(copy(other_ref, slot).start)
    base = base_ref[layer] if first else base_ref[...]
    total_ref[...] = base.astype(jnp.float32)
    if len(blocks_refs) == 1:
        assemble(blocks_refs[0], full_ref, 0)
    else:
        for side, blocks_ref in enumerate(blocks_refs):
            pl.when(core == side)(functools.partial(assemble, blocks_ref, full_ref, side))

    def subtract(slot, _):
        @pl.when(jnp.max(plan_ref[layer, slot]) == kind)
        def _():
            copy(own_ref, slot).wait()
            real, imag = complex_parts(multiply(full_ref[...], weights[slot]))
            cosine = jnp.broadcast_to(table_ref[layer, slot, 0][:, :1], (cols, rows))
            sine = jnp.broadcast_to(table_ref[layer, slot, 1][:, :1], (cols, rows))
            total_ref[:cols] -= real * cosine - imag * sine
            total_ref[cols:] -= real * sine + imag * cosine

        return 0

    lax.fori_loop(0, slots, subtract, 0)
    if out_ref.ndim == 2:
        out_ref[...] = total_ref[...]
    else:
        total = total_ref[...].astype(jnp.bfloat16)
        for place in range(out_ref.shape[0]):
            out_ref[place] = total


def inverse_kernel(weight_ref, blocks_ref, *refs):
    parts = sum(ref.ndim == 2 for ref in refs[:-1])
    field_refs, copied_refs, full_ref = refs[:parts], refs[parts:-1], refs[-1]
    assemble(blocks_ref, full_ref, 0)
    real, imag = complex_parts(multiply(full_ref[...], weight_ref[...]))
    real, imag = real.astype(jnp.bfloat16), imag.astype(jnp.bfloat16)
    cols = real.shape[0]
    half = cols // parts
    for part, field_ref in enumerate(field_refs):
        field_ref[:half] = real[part * half : (part + 1) * half]
        field_ref[half:] = imag[part * half : (part + 1) * half]
    for copied_ref in copied_refs:
        for place in range(copied_ref.shape[0]):
            copied_ref[place, :cols] = real
            copied_ref[place, cols:] = imag


def nothing(shapes):
    return list(
        pl.pallas_call(
            lambda *refs: None, out_shape=shapes, out_specs=[ANY] * len(shapes), name="nothing"
        )()
    )


def held(array):
    return pltpu.with_memory_space_constraint(array, pltpu.VMEM)


def far(array):
    return pltpu.with_memory_space_constraint(array, pltpu.HBM)


def local(right_side, inverse, coupling, image_offset, image_count, phase_exponent):
    layers, rows, _, cols = right_side.shape
    slots, unknowns = coupling.shape[1], coupling.shape[4]
    peers = lax.axis_size("angle")
    chips = lax.axis_size("layer") // CORES
    chip, core = jnp.divmod(lax.axis_index("layer"), CORES)
    deep = CORES * layers
    width = cols // CORES
    wide = 2 * width

    def ordered(mine, given):
        return jnp.where(core == 0, jnp.concatenate([mine, given]), jnp.concatenate([given, mine]))

    right = right_side.reshape(layers, rows, 2, CORES, width).transpose(3, 0, 2, 4, 1)
    split = right.reshape(CORES, layers, wide, rows)
    right = ordered(
        jnp.where(core == 0, split[0], split[1]), swap(jnp.where(core == 0, split[1], split[0]))
    )
    kinds = jnp.where(lax.iota(jnp.int32, slots) < image_count[:, None], image_offset, 0)
    both = jnp.stack([kinds, phase_exponent], 1)
    both = ordered(both, swap(both))
    begin = right_side[0].transpose(1, 2, 0).reshape(CORES * wide, rows)
    tied = lax.optimization_barrier((right, both, begin, inverse, coupling))
    right, both, begin, late_inverse, late_coupling = tied
    other_coupling, other_inverse = swap(late_coupling), swap(late_inverse)
    plan = jnp.concatenate([both[:, 0], jnp.full((1, slots), core, jnp.int32)]).astype(jnp.float32)
    plan = jnp.broadcast_to(plan[..., None, None], (deep + 1, slots, 8, 128))
    angle = ((core * width + lax.iota(jnp.int32, width)) // NRHS).astype(jnp.float32)
    phase = (2.0 * math.pi / ANGLES) * both[:, 1].astype(jnp.float32)[:, :, None] * (angle + 0.5)
    table = jnp.stack([jnp.cos(phase), jnp.sin(phase)], 2)
    table = jnp.broadcast_to(table[..., None], table.shape + (128,))

    params = pltpu.CompilerParams(vmem_limit_bytes=LIMIT)
    field_shape = jax.ShapeDtypeStruct((wide, rows), jnp.bfloat16)
    copied_shape = jax.ShapeDtypeStruct((peers, wide, rows), jnp.bfloat16)
    full_scratch = pltpu.VMEM((wide, unknowns), jnp.bfloat16)

    def cost(planes):
        return pl.CostEstimate(
            flops=4 * wide * rows * unknowns * planes,
            bytes_accessed=4 * rows * unknowns * planes,
            transcendentals=0,
        )

    def images(layer, kind, base, blocks):
        return pl.pallas_call(
            functools.partial(image_kernel, layer, kind, base.ndim == 3),
            out_shape=copied_shape if kind == 1 else jax.ShapeDtypeStruct((wide, rows), jnp.float32),
            in_specs=[VMEM] * 2 + [ANY] * 2 + [VMEM] * (1 + len(blocks)),
            out_specs=VMEM,
            scratch_shapes=[
                pltpu.VMEM((wide, rows), jnp.float32),
                full_scratch,
                pltpu.VMEM((slots, 2, rows, unknowns), jnp.bfloat16),
                pltpu.SemaphoreType.DMA((slots,)),
            ],
            compiler_params=params,
            cost_estimate=cost(slots // 2),
            name="images_%d" % kind,
        )(plan, table, far(coupling), far(other_coupling), base, *blocks)

    def invert(blocks, weights, last):
        parts = blocks.shape[1] // wide
        out_shape = [field_shape] * parts + [jax.ShapeDtypeStruct(blocks.shape, jnp.bfloat16)] * (not last)
        return pl.pallas_call(
            inverse_kernel,
            out_shape=out_shape,
            in_specs=[VMEM] * 2,
            out_specs=[VMEM] * len(out_shape),
            scratch_shapes=[pltpu.VMEM((parts * wide, unknowns), jnp.bfloat16)],
            compiler_params=params,
            cost_estimate=cost(1),
            name="invert",
        )(held(weights), blocks)

    def load(layer, other, after):
        return pl.pallas_call(
            functools.partial(load_kernel, layer),
            out_shape=pltpu.VMEM(inverse.shape[1:], inverse.dtype),
            in_specs=[VMEM] + [ANY] * 3,
            out_specs=VMEM,
            scratch_shapes=[pltpu.SemaphoreType.DMA],
            compiler_params=pltpu.CompilerParams(vmem_limit_bytes=2**20),
            cost_estimate=pl.CostEstimate(flops=0, bytes_accessed=inverse.size * 2, transcendentals=0),
            name="load",
        )(plan, far(inverse), far(other), after)

    def run(start, latest, earlier):
        fields = []
        for layer in range(start, deep):
            base = right if earlier is None else images(layer, 2, right, earlier)
            copied = images(layer, 1, base, latest)
            if layer + 1 < deep:
                field, next_copied = invert(gather(copied), load(layer, other_inverse, copied), False)
                fields.append(field)
                earlier, latest = latest, [gather(next_copied)]
        return [*fields, copied, *latest]

    def finish(copied):
        return list(invert(gather(copied), load(deep - 1, other_inverse, copied), True))

    def only(here, shapes, function, *operands):
        return lax.cond(here, function, lambda *_: nothing(shapes), *operands)

    found = []
    field = earlier = None
    for number in range(chips):
        if number == 0:
            gathered = jax.ShapeDtypeStruct((peers, CORES * wide, rows), jnp.bfloat16)

            def layer_zero(begin):
                copied = copies(begin, peers)
                *fields, copied = invert(gather(copied), load(0, inverse, copied), False)
                return [*fields, gather(copied)]

            begin, _ = lax.optimization_barrier((begin, table))
            shapes = [field_shape] * CORES + [gathered]
            *zero, latest = only((chip == 0) & (core == 0), shapes, layer_zero, begin)
            pairs = [(b, peers + b) for b in range(peers)]
            given = lax.ppermute(latest, ("layer", "angle"), pairs)
            start, function, operands = 1, lambda *latest: run(1, latest, None), (latest, given)
        else:

            def function(field, earlier):
                return run(0, [gather(copies(field, peers))], [earlier])

            start, operands = 0, (field, earlier)
        here = chip == number
        shapes = [field_shape] * (deep - start - 1) + [copied_shape] * 2
        *fields, copied, latest = only(here, shapes, function, *operands)
        if number + 1 < chips:
            earlier = shift(latest, number)
        (last,) = only(here, [field_shape], finish, copied)
        found.append((zero[:1] if start else []) + fields + [last])
        if number + 1 < chips:
            field = shift(last, number)

    chosen = []
    for layer in range(deep):
        value = found[0][layer]
        for number in range(1, chips):
            value = jnp.where(chip == number, found[number][layer], value)
        chosen.append(value)
    low, high = jnp.stack(chosen[:layers]), jnp.stack(chosen[layers:])
    mine = jnp.where(core == 0, low, high)
    given = swap(jnp.where(core == 0, high, low))
    first_given = jnp.where(chip == 0, jnp.where(core == 0, zero[1], given[0]), given[0])
    given = jnp.concatenate([first_given[None], given[1:]])
    result = jnp.where(core == 0, jnp.stack([mine, given]), jnp.stack([given, mine]))
    result = result.reshape(CORES, layers, 2, width, rows).transpose(1, 4, 2, 0, 3)
    return result.reshape(layers, rows, 2, cols)


def solution(mesh):
    placed = (
        P("layer", "angle", None, None),
        P("layer", None, "angle", None),
        P("layer", None, None, "angle", None),
        P("layer", None),
        P("layer"),
        P("layer", None),
    )
    return jax.shard_map(
        local,
        mesh=mesh,
        in_specs=placed,
        out_specs=P("layer", "angle", None, None),
        check_vma=False,
    )
```

profile of v0, /device:TPU:3, one launch (start us, length us, event | category | flops | bytes accessed | tf_op | source)
XLA Modules:
  0.0 291.7 jit_solution(12883926740114705718)
XLA Ops:
  8.8 27.7 %collective-permute-done.4 = bf16[2,2,256,2048]{3,2,1,0:T(8,128)(2,1)} collective-permute-done((bf16[2,2,256,2048]{3,2,1,0:T(8,128)(2,1)}, bf16[2,2,256,2048]{3,2,1,0:T(8,128)(2,1)}, u32[]{:S(2)}, u32[]{:S(2)}) %collective-permute-start.4) | collective-permute-done | bytes 4194336 | tf_op jit(solution)/shard_map/ppermute | solution.py:38
  39.3 108.3 %collective-permute-done.6 = bf16[96,256]{1,0:T(8,128)(2,1)S(1)} collective-permute-done((bf16[96,256]{1,0:T(8,128)(2,1)}, bf16[96,256]{1,0:T(8,128)(2,1)S(1)}, u32[]{:S(2)}, u32[]{:S(2)}) %collective-permute-start.6) | collective-permute-done | bytes 49184 | tf_op jit(solution)/shard_map/ppermute | solution.py:44
  147.7 122.8 %conditional.8 = (bf16[96,256]{1,0:T(8,128)(2,1)}, bf16[96,256]{1,0:T(8,128)(2,1)}, bf16[96,256]{1,0:T(8,128)(2,1)}, bf16[8,96,256]{2,1,0:T(8,128)(2,1)}) conditional(s32[]{:T(128)} %convert_element_type.29, () %tuple.43, (f32[5,4,8,128]{3,2,1,0:T(8,128)S(1)}, f32[4,4,2,48,128]{4,3,2,1,0:T(8,128)S(1)}, bf16[2,4,2,256,2048]{4,3,2,1,0:T(8,128)(2,1)}, ...), branch_computations={%region_6.7_spmd, %region_7.8_spmd} | conditional | flops 3825205248 | bytes 73269616 | solution.py:266
  148.5 5.7 %all-to-all-start.7 = ((bf16[8,96,256]{2,1,0:T(8,128)(2,1)}), bf16[8,96,256]{2,1,0:T(8,128)(2,1)S(1)}, u32[]{:S(2)}, u32[]{:S(2)}) async-start(bf16[8,96,256]{2,1,0:T(8,128)(2,1)} %copies.3), calls=%async_computation.7 | async-start | bytes 786432 | tf_op jit(solution)/shard_map/cond/branch_1_fun/all_to_all | solution.py:48
  154.3 5.5 %images_2.8.base_ref = f32[96,256]{1,0:T(8,128)S(1)} custom-call(f32[5,4,8,128]{3,2,1,0:T(8,128)S(1)} %get-tuple-element.96.plan_ref, f32[4,4,2,48,128]{4,3,2,1,0:T(8,128)S(1)} %get-tuple-element.99.table_ref, bf16[2,4,2,256,2048]{4,3,2,1,0:T(8,128)(2,1)} %get-tuple-element.100.own_ref, bf16[2,4,2,256,2048]{4,3,2,1,0:T(8,128)(2,1)} %get-tuple-element.101.other_ref, ...), custom_call_target="tpu_custom_call" | custom-call | flops 402653184 | bytes 4194304 | tf_op jit(solution)/shard_map/cond/branch_1_fun/images_2/pallas_call | solution.py:209
  165.7 6.4 %all-to-all-start.8 = ((bf16[8,96,256]{2,1,0:T(8,128)(2,1)}), bf16[8,96,256]{2,1,0:T(8,128)(2,1)S(1)}, u32[]{:S(2)}, u32[]{:S(2)}) async-start(bf16[8,96,256]{2,1,0:T(8,128)(2,1)} %images_1.10._), calls=%async_computation.8 | async-start | bytes 786432 | tf_op jit(solution)/shard_map/cond/branch_1_fun/all_to_all | solution.py:48
  173.8 6.6 %all-to-all-done.8.blocks_ref = bf16[8,96,256]{2,1,0:T(8,128)(2,1)S(1)} async-done(((bf16[8,96,256]{2,1,0:T(8,128)(2,1)}), bf16[8,96,256]{2,1,0:T(8,128)(2,1)S(1)}, u32[]{:S(2)}, u32[]{:S(2)}) %all-to-all-start.8) | async-done | bytes 393248 | tf_op jit(solution)/shard_map/cond/branch_1_fun/all_to_all | solution.py:48
  182.0 6.5 %all-to-all-start.9 = ((bf16[8,96,256]{2,1,0:T(8,128)(2,1)}), bf16[8,96,256]{2,1,0:T(8,128)(2,1)S(1)}, u32[]{:S(2)}, u32[]{:S(2)}) async-start(bf16[8,96,256]{2,1,0:T(8,128)(2,1)} %get-tuple-element.106), calls=%async_computation.9 | async-start | bytes 786432 | tf_op jit(solution)/shard_map/cond/branch_1_fun/all_to_all | solution.py:48
  188.5 4.2 %images_2.9.base_ref = f32[96,256]{1,0:T(8,128)S(1)} custom-call(f32[5,4,8,128]{3,2,1,0:T(8,128)S(1)} %get-tuple-element.96.plan_ref, f32[4,4,2,48,128]{4,3,2,1,0:T(8,128)} %copy-done.3, bf16[2,4,2,256,2048]{4,3,2,1,0:T(8,128)(2,1)} %get-tuple-element.100.own_ref, bf16[2,4,2,256,2048]{4,3,2,1,0:T(8,128)(2,1)} %get-tuple-element.101.other_ref, ...), custom_call_target="tpu_custom_call" | custom-call | flops 402653184 | bytes 4194304 | tf_op jit(solution)/shard_map/cond/branch_1_fun/images_2/pallas_call | solution.py:209
  192.7 4.9 %all-to-all-done.9.refs_0_ = bf16[8,96,256]{2,1,0:T(8,128)(2,1)S(1)} async-done(((bf16[8,96,256]{2,1,0:T(8,128)(2,1)}), bf16[8,96,256]{2,1,0:T(8,128)(2,1)S(1)}, u32[]{:S(2)}, u32[]{:S(2)}) %all-to-all-start.9) | async-done | bytes 393248 | tf_op jit(solution)/shard_map/cond/branch_1_fun/all_to_all | solution.py:48
  197.5 4.4 %images_1.11._ = bf16[8,96,256]{2,1,0:T(8,128)(2,1)} custom-call(f32[5,4,8,128]{3,2,1,0:T(8,128)S(1)} %get-tuple-element.96.plan_ref, f32[4,4,2,48,128]{4,3,2,1,0:T(8,128)S(1)} %copy-done.4, bf16[2,4,2,256,2048]{4,3,2,1,0:T(8,128)(2,1)} %get-tuple-element.100.own_ref, bf16[2,4,2,256,2048]{4,3,2,1,0:T(8,128)(2,1)} %get-tuple-element.101.other_ref, ...), custom_call_target="tpu_custom_call" | custom-call | flops 402653184 | bytes 4194304 | tf_op jit(solution)/shard_map/cond/branch_1_fun/images_1/pallas_call | solution.py:209
  201.9 5.7 %all-to-all-start.10 = ((bf16[8,96,256]{2,1,0:T(8,128)(2,1)}), bf16[8,96,256]{2,1,0:T(8,128)(2,1)S(1)}, u32[]{:S(2)}, u32[]{:S(2)}) async-start(bf16[8,96,256]{2,1,0:T(8,128)(2,1)} %images_1.11._), calls=%async_computation.10 | async-start | bytes 786432 | tf_op jit(solution)/shard_map/cond/branch_1_fun/all_to_all | solution.py:48
  209.4 7.3 %all-to-all-done.10.blocks_ref = bf16[8,96,256]{2,1,0:T(8,128)(2,1)S(1)} async-done(((bf16[8,96,256]{2,1,0:T(8,128)(2,1)}), bf16[8,96,256]{2,1,0:T(8,128)(2,1)S(1)}, u32[]{:S(2)}, u32[]{:S(2)}) %all-to-all-start.10) | async-done | bytes 393248 | tf_op jit(solution)/shard_map/cond/branch_1_fun/all_to_all | solution.py:48
  218.3 5.7 %all-to-all-start.11 = ((bf16[8,96,256]{2,1,0:T(8,128)(2,1)}), bf16[8,96,256]{2,1,0:T(8,128)(2,1)S(1)}, u32[]{:S(2)}, u32[]{:S(2)}) async-start(bf16[8,96,256]{2,1,0:T(8,128)(2,1)} %get-tuple-element.108), calls=%async_computation.11 | async-start | bytes 786432 | tf_op jit(solution)/shard_map/cond/branch_1_fun/all_to_all | solution.py:48
  228.1 5.0 %all-to-all-done.11.refs_0_ = bf16[8,96,256]{2,1,0:T(8,128)(2,1)S(1)} async-done(((bf16[8,96,256]{2,1,0:T(8,128)(2,1)}), bf16[8,96,256]{2,1,0:T(8,128)(2,1)S(1)}, u32[]{:S(2)}, u32[]{:S(2)}) %all-to-all-start.11) | async-done | bytes 393248 | tf_op jit(solution)/shard_map/cond/branch_1_fun/all_to_all | solution.py:48
  233.1 4.5 %images_1.12._ = bf16[8,96,256]{2,1,0:T(8,128)(2,1)} custom-call(f32[5,4,8,128]{3,2,1,0:T(8,128)S(1)} %get-tuple-element.96.plan_ref, f32[4,4,2,48,128]{4,3,2,1,0:T(8,128)S(1)} %copy-done.5, bf16[2,4,2,256,2048]{4,3,2,1,0:T(8,128)(2,1)} %get-tuple-element.100.own_ref, bf16[2,4,2,256,2048]{4,3,2,1,0:T(8,128)(2,1)} %get-tuple-element.101.other_ref, ...), custom_call_target="tpu_custom_call" | custom-call | flops 402653184 | bytes 4194304 | tf_op jit(solution)/shard_map/cond/branch_1_fun/images_1/pallas_call | solution.py:209
  237.6 5.7 %all-to-all-start.12 = ((bf16[8,96,256]{2,1,0:T(8,128)(2,1)}), bf16[8,96,256]{2,1,0:T(8,128)(2,1)S(1)}, u32[]{:S(2)}, u32[]{:S(2)}) async-start(bf16[8,96,256]{2,1,0:T(8,128)(2,1)} %images_1.12._), calls=%async_computation.12 | async-start | bytes 786432 | tf_op jit(solution)/shard_map/cond/branch_1_fun/all_to_all | solution.py:48
  245.1 7.3 %all-to-all-done.12.blocks_ref = bf16[8,96,256]{2,1,0:T(8,128)(2,1)S(1)} async-done(((bf16[8,96,256]{2,1,0:T(8,128)(2,1)}), bf16[8,96,256]{2,1,0:T(8,128)(2,1)S(1)}, u32[]{:S(2)}, u32[]{:S(2)}) %all-to-all-start.12) | async-done | bytes 393248 | tf_op jit(solution)/shard_map/cond/branch_1_fun/all_to_all | solution.py:48
  254.0 5.7 %all-to-all-start.13 = ((bf16[8,96,256]{2,1,0:T(8,128)(2,1)}), bf16[8,96,256]{2,1,0:T(8,128)(2,1)S(1)}, u32[]{:S(2)}, u32[]{:S(2)}) async-start(bf16[8,96,256]{2,1,0:T(8,128)(2,1)} %get-tuple-element.110), calls=%async_computation.13 | async-start | bytes 786432 | tf_op jit(solution)/shard_map/cond/branch_1_fun/all_to_all | solution.py:48
  259.7 4.9 %images_2.11.base_ref = f32[96,256]{1,0:T(8,128)S(1)} custom-call(f32[5,4,8,128]{3,2,1,0:T(8,128)S(1)} %get-tuple-element.96.plan_ref, f32[4,4,2,48,128]{4,3,2,1,0:T(8,128)} %copy-done.3, bf16[2,4,2,256,2048]{4,3,2,1,0:T(8,128)(2,1)} %get-tuple-element.100.own_ref, bf16[2,4,2,256,2048]{4,3,2,1,0:T(8,128)(2,1)} %get-tuple-element.101.other_ref, ...), custom_call_target="tpu_custom_call" | custom-call | flops 402653184 | bytes 4194304 | tf_op jit(solution)/shard_map/cond/branch_1_fun/images_2/pallas_call | solution.py:209
  264.7 4.1 %all-to-all-done.13.refs_0_ = bf16[8,96,256]{2,1,0:T(8,128)(2,1)S(1)} async-done(((bf16[8,96,256]{2,1,0:T(8,128)(2,1)}), bf16[8,96,256]{2,1,0:T(8,128)(2,1)S(1)}, u32[]{:S(2)}, u32[]{:S(2)}) %all-to-all-start.13) | async-done | bytes 393248 | tf_op jit(solution)/shard_map/cond/branch_1_fun/all_to_all | solution.py:48
  270.5 15.7 %conditional.9 = (bf16[96,256]{1,0:T(8,128)(2,1)S(1)}) conditional(s32[]{:T(128)} %convert_element_type.29, () %tuple.53, (f32[5,4,8,128]{3,2,1,0:T(8,128)S(1)}, bf16[2,2,256,2048]{3,2,1,0:T(8,128)(2,1)}, bf16[2,2,256,2048]{3,2,1,0:T(8,128)(2,1)}, bf16[8,96,256]{2,1,0:T(8,128)(2,1)}) %tuple.54), branch_computations={%region_8.9_spmd, %region_9.10_spmd} | conditional | flops 201326592 | bytes 7471144 | solution.py:266
  270.6 5.9 %all-to-all-start.14 = ((bf16[8,96,256]{2,1,0:T(8,128)(2,1)}), bf16[8,96,256]{2,1,0:T(8,128)(2,1)S(1)}, u32[]{:S(2)}, u32[]{:S(2)}) async-start(bf16[8,96,256]{2,1,0:T(8,128)(2,1)} %get-tuple-element.114._), calls=%async_computation.14 | async-start | bytes 786432 | tf_op jit(solution)/shard_map/cond/branch_1_fun/all_to_all | solution.py:48
  278.2 7.3 %all-to-all-done.14.blocks_ref = bf16[8,96,256]{2,1,0:T(8,128)(2,1)S(1)} async-done(((bf16[8,96,256]{2,1,0:T(8,128)(2,1)}), bf16[8,96,256]{2,1,0:T(8,128)(2,1)S(1)}, u32[]{:S(2)}, u32[]{:S(2)}) %all-to-all-start.14) | async-done | bytes 393248 | tf_op jit(solution)/shard_map/cond/branch_1_fun/all_to_all | solution.py:48
  (78 shorter events, 41.6 us)
Async XLA Ops:
  1.4 2.6 collective-permute-start.1
  3.1 1.8 collective-permute-start
  4.9 31.7 %collective-permute-start.2 = (bf16[2,4,2,256,2048]{4,3,2,1,0:T(8,128)(2,1)}, bf16[2,4,2,256,2048]{4,3,2,1,0:T(8,128)(2,1)}, u32[]{:S(2)}, u32[]{:S(2)}) collective-permute-start(bf16[2,4,2,256,2048]{4,3,2,1,0:T(8,128)(2,1)} %param.18), channel_id=1, source_target_pairs={{0,8},{8,0},{16,24},{24,16},{1,9},{9,1},{17,25},{25,17},{2,10},{10... | collective-permute-start | bytes 50331656 | tf_op jit(solution)/shard_map/ppermute | solution.py:38
  5.4 31.1 %collective-permute-start.4 = (bf16[2,2,256,2048]{3,2,1,0:T(8,128)(2,1)}, bf16[2,2,256,2048]{3,2,1,0:T(8,128)(2,1)}, u32[]{:S(2)}, u32[]{:S(2)}) collective-permute-start(bf16[2,2,256,2048]{3,2,1,0:T(8,128)(2,1)} %param.17), channel_id=1, source_target_pairs={{0,8},{8,0},{16,24},{24,16},{1,9},{9,1},{17,25},{25,17},{2,10},{10... | collective-permute-start | bytes 12582920 | tf_op jit(solution)/shard_map/ppermute | solution.py:38
  8.1 0.7 collective-permute-start.3
  36.5 111.1 %collective-permute-start.5 = (bf16[8,96,256]{2,1,0:T(8,128)(2,1)}, bf16[8,96,256]{2,1,0:T(8,128)(2,1)}, u32[]{:S(2)}, u32[]{:S(2)}) collective-permute-start(bf16[8,96,256]{2,1,0:T(8,128)(2,1)} %get-tuple-element.139), channel_id=1, source_target_pairs={{0,16},{1,17},{2,18},{3,19},{4,20},{5,21},{6,22},{7,23},{8,24},{9,... | collective-permute-start | bytes 1179656 | tf_op jit(solution)/shard_map/ppermute | solution.py:44
  37.8 109.8 %copy-start = (f32[4,4,2,48,128]{4,3,2,1,0:T(8,128)S(1)}, f32[4,4,2,48,128]{4,3,2,1,0:T(8,128)}, u32[]{:S(2)}) copy-start(f32[4,4,2,48,128]{4,3,2,1,0:T(8,128)} %broadcast_in_dim.10) | copy-start | bytes 2359300
  37.9 109.8 %collective-permute-start.6 = (bf16[96,256]{1,0:T(8,128)(2,1)}, bf16[96,256]{1,0:T(8,128)(2,1)S(1)}, u32[]{:S(2)}, u32[]{:S(2)}) collective-permute-start(bf16[96,256]{1,0:T(8,128)(2,1)} %get-tuple-element.181), channel_id=1, source_target_pairs={{0,16},{1,17},{2,18},{3,19},{4,20},{5,21},{6,22},{7,23},{8,24},{9,... | collective-permute-start | bytes 147464 | tf_op jit(solution)/shard_map/ppermute | solution.py:44
  147.7 14.7 %copy-start.3 = (f32[4,4,2,48,128]{4,3,2,1,0:T(8,128)}, f32[4,4,2,48,128]{4,3,2,1,0:T(8,128)S(1)}, u32[]{:S(2)}) copy-start(f32[4,4,2,48,128]{4,3,2,1,0:T(8,128)S(1)} %get-tuple-element.99.table_ref) | copy-start | bytes 2359300 | tf_op jit(solution)/shard_map/cond
  148.5 13.8 %all-to-all-start.7 = ((bf16[8,96,256]{2,1,0:T(8,128)(2,1)}), bf16[8,96,256]{2,1,0:T(8,128)(2,1)S(1)}, u32[]{:S(2)}, u32[]{:S(2)}) async-start(bf16[8,96,256]{2,1,0:T(8,128)(2,1)} %copies.3), calls=%async_computation.7 | async-start | bytes 786432 | tf_op jit(solution)/shard_map/cond/branch_1_fun/all_to_all | solution.py:48
  165.7 14.7 %all-to-all-start.8 = ((bf16[8,96,256]{2,1,0:T(8,128)(2,1)}), bf16[8,96,256]{2,1,0:T(8,128)(2,1)S(1)}, u32[]{:S(2)}, u32[]{:S(2)}) async-start(bf16[8,96,256]{2,1,0:T(8,128)(2,1)} %images_1.10._), calls=%async_computation.8 | async-start | bytes 786432 | tf_op jit(solution)/shard_map/cond/branch_1_fun/all_to_all | solution.py:48
  182.0 15.5 %all-to-all-start.9 = ((bf16[8,96,256]{2,1,0:T(8,128)(2,1)}), bf16[8,96,256]{2,1,0:T(8,128)(2,1)S(1)}, u32[]{:S(2)}, u32[]{:S(2)}) async-start(bf16[8,96,256]{2,1,0:T(8,128)(2,1)} %get-tuple-element.106), calls=%async_computation.9 | async-start | bytes 786432 | tf_op jit(solution)/shard_map/cond/branch_1_fun/all_to_all | solution.py:48
  188.5 9.1 %copy-start.4 = (f32[4,4,2,48,128]{4,3,2,1,0:T(8,128)S(1)}, f32[4,4,2,48,128]{4,3,2,1,0:T(8,128)}, u32[]{:S(2)}) copy-start(f32[4,4,2,48,128]{4,3,2,1,0:T(8,128)} %copy-done.3) | copy-start | bytes 2359300 | tf_op jit(solution)/shard_map/cond
  201.9 14.8 %all-to-all-start.10 = ((bf16[8,96,256]{2,1,0:T(8,128)(2,1)}), bf16[8,96,256]{2,1,0:T(8,128)(2,1)S(1)}, u32[]{:S(2)}, u32[]{:S(2)}) async-start(bf16[8,96,256]{2,1,0:T(8,128)(2,1)} %images_1.11._), calls=%async_computation.10 | async-start | bytes 786432 | tf_op jit(solution)/shard_map/cond/branch_1_fun/all_to_all | solution.py:48
  218.3 14.8 %all-to-all-start.11 = ((bf16[8,96,256]{2,1,0:T(8,128)(2,1)}), bf16[8,96,256]{2,1,0:T(8,128)(2,1)S(1)}, u32[]{:S(2)}, u32[]{:S(2)}) async-start(bf16[8,96,256]{2,1,0:T(8,128)(2,1)} %get-tuple-element.108), calls=%async_computation.11 | async-start | bytes 786432 | tf_op jit(solution)/shard_map/cond/branch_1_fun/all_to_all | solution.py:48
  237.6 14.8 %all-to-all-start.12 = ((bf16[8,96,256]{2,1,0:T(8,128)(2,1)}), bf16[8,96,256]{2,1,0:T(8,128)(2,1)S(1)}, u32[]{:S(2)}, u32[]{:S(2)}) async-start(bf16[8,96,256]{2,1,0:T(8,128)(2,1)} %images_1.12._), calls=%async_computation.12 | async-start | bytes 786432 | tf_op jit(solution)/shard_map/cond/branch_1_fun/all_to_all | solution.py:48
  254.0 14.8 %all-to-all-start.13 = ((bf16[8,96,256]{2,1,0:T(8,128)(2,1)}), bf16[8,96,256]{2,1,0:T(8,128)(2,1)S(1)}, u32[]{:S(2)}, u32[]{:S(2)}) async-start(bf16[8,96,256]{2,1,0:T(8,128)(2,1)} %get-tuple-element.110), calls=%async_computation.13 | async-start | bytes 786432 | tf_op jit(solution)/shard_map/cond/branch_1_fun/all_to_all | solution.py:48
  270.5 15.8 %copy-start.12 = (bf16[96,256]{1,0:T(8,128)(2,1)S(1)}, bf16[96,256]{1,0:T(8,128)(2,1)}, u32[]{:S(2)}) copy-start(bf16[96,256]{1,0:T(8,128)(2,1)} %get-tuple-element.145) | copy-start | bytes 147460
  270.5 15.8 %copy-start.10 = (bf16[96,256]{1,0:T(8,128)(2,1)S(1)}, bf16[96,256]{1,0:T(8,128)(2,1)}, u32[]{:S(2)}) copy-start(bf16[96,256]{1,0:T(8,128)(2,1)} %get-tuple-element.141) | copy-start | bytes 147460
  270.5 15.8 %copy-start.11 = (bf16[96,256]{1,0:T(8,128)(2,1)S(1)}, bf16[96,256]{1,0:T(8,128)(2,1)}, u32[]{:S(2)}) copy-start(bf16[96,256]{1,0:T(8,128)(2,1)} %get-tuple-element.143) | copy-start | bytes 147460
  270.5 15.8 %copy-start.13 = (bf16[96,256]{1,0:T(8,128)(2,1)S(1)}, bf16[96,256]{1,0:T(8,128)(2,1)}, u32[]{:S(2)}) copy-start(bf16[96,256]{1,0:T(8,128)(2,1)} %get-tuple-element.142) | copy-start | bytes 147460
  270.5 20.5 %copy-start.14 = (bf16[96,256]{1,0:T(8,128)(2,1)S(1)}, bf16[96,256]{1,0:T(8,128)(2,1)}, u32[]{:S(2)}) copy-start(bf16[96,256]{1,0:T(8,128)(2,1)} %get-tuple-element.148) | copy-start | bytes 147460
  270.6 14.9 %all-to-all-start.14 = ((bf16[8,96,256]{2,1,0:T(8,128)(2,1)}), bf16[8,96,256]{2,1,0:T(8,128)(2,1)S(1)}, u32[]{:S(2)}, u32[]{:S(2)}) async-start(bf16[8,96,256]{2,1,0:T(8,128)(2,1)} %get-tuple-element.114._), calls=%async_computation.14 | async-start | bytes 786432 | tf_op jit(solution)/shard_map/cond/branch_1_fun/all_to_all | solution.py:48
  286.4 4.6 %collective-permute-start.7 = (bf16[2,96,256]{2,1,0:T(8,128)(2,1)S(1)}, bf16[2,96,256]{2,1,0:T(8,128)(2,1)S(1)}, u32[]{:S(2)}, u32[]{:S(2)}) collective-permute-start(bf16[2,96,256]{2,1,0:T(8,128)(2,1)S(1)} %maximum_select_fusion.3), channel_id=1, source_target_pairs={{0,8},{8,0},{16,24},{24,16},{1,9},{9,1},{17,25},{25,17},{2,10},{10... | collective-permute-start | bytes 294920 | tf_op jit(solution)/shard_map/ppermute | solution.py:38
  (4 other events, 20.3 us)
where the time goes:
time: 292 us
  waiting for transfers between devices  182 us (62%)
  starting transfers between devices  55.8 us (19%)
  Pallas kernels  45.5 us (16%)
  other arithmetic  4.34 us (1%)
  local copies, waits for them, and re-layouts  3.1 us (1%)
    ppermute x2, waiting for transfers between devices, shift(): lax.ppermute(array, ('layer', 'angle'), [(i, i + CORES * peers) for i in...  108 us
    all_to_all x8, starting transfers between devices, gather(): return lax.all_to_all(copied, 'angle', 0, 0)  47.4 us
    all_to_all x8, waiting for transfers between devices, gather(): return lax.all_to_all(copied, 'angle', 0, 0)  45.2 us
    pallas_call x8, Pallas kernels, images(): pl.pallas_call(functools.partial(image_kernel, layer, kind, base.ndim ==...  32.3 us
    ppermute x5, waiting for transfers between devices, swap(): return lax.ppermute(array, 'layer', pairs)  28.7 us
    pallas_call x4, Pallas kernels, load(): pl.pallas_call(functools.partial(load_kernel, layer), out_shape=pltpu.VME...  6.86 us
  transfers between devices with their start and end apart: 16, of which 11 were waited for; matrix products, arithmetic and copies ran while one was open for 1% of the time, Pallas kernels for 9%

commit v1 on v0

--- a/solution.py
+++ b/solution.py
@@ -84,8 +84,13 @@
     mine.wait()
 
 
-def image_kernel(layer, kind, first, plan_ref, table_ref, own_ref, other_ref, base_ref, *refs):
+def image_kernel(layer, kind, first, ahead, plan_ref, table_ref, own_ref, other_ref, base_ref, *refs):
     *blocks_refs, out_ref, total_ref, full_ref, weights, sems = refs
+    ahead_ref = None
+    if ahead and kind == 1:
+        ahead_ref = blocks_refs.pop()
+    elif ahead:
+        out_ref, ahead_ref = blocks_refs.pop(), out_ref
     wide, rows = total_ref.shape
     cols = wide // 2
     layers, slots = own_ref.shape[:2]
@@ -95,10 +100,23 @@
     def copy(weight_ref, slot):
         return pltpu.make_async_copy(weight_ref.at[layer % layers, slot], weights.at[slot], sems.at[slot])
 
+    found = jnp.int32(0)
     for slot in range(slots):
         used = jnp.max(plan_ref[layer, slot]) == kind
-        pl.when(used & own)(copy(own_ref, slot).start)
-        pl.when(used & jnp.logical_not(own))(copy(other_ref, slot).start)
+        wanted = used & (found > 0) if ahead and kind == 1 else used
+        pl.when(wanted & own)(copy(own_ref, slot).start)
+        pl.when(wanted & jnp.logical_not(own))(copy(other_ref, slot).start)
+        found = found + used.astype(jnp.int32)
+    if ahead and kind == 2:
+        next_found = jnp.int32(0)
+        for slot in range(slots):
+            used = jnp.max(plan_ref[layer, slot]) == 1
+            wanted = used & (next_found == 0)
+            for mine, weight_ref in ((own, own_ref), (jnp.logical_not(own), other_ref)):
+                source = weight_ref.at[layer % layers, slot]
+                fetch = pltpu.make_async_copy(source, ahead_ref, sems.at[slots])
+                pl.when(wanted & mine)(fetch.start)
+            next_found = next_found + used.astype(jnp.int32)
     base = base_ref[layer] if first else base_ref[...]
     total_ref[...] = base.astype(jnp.float32)
     if len(blocks_refs) == 1:
@@ -107,19 +125,33 @@
         for side, blocks_ref in enumerate(blocks_refs):
             pl.when(core == side)(functools.partial(assemble, blocks_ref, full_ref, side))
 
-    def subtract(slot, _):
-        @pl.when(jnp.max(plan_ref[layer, slot]) == kind)
+    def subtract(slot, weight):
+        real, imag = complex_parts(multiply(full_ref[...], weight))
+        cosine = jnp.broadcast_to(table_ref[layer, slot, 0][:, :1], (cols, rows))
+        sine = jnp.broadcast_to(table_ref[layer, slot, 1][:, :1], (cols, rows))
+        total_ref[:cols] -= real * cosine - imag * sine
+        total_ref[cols:] -= real * sine + imag * cosine
+
+    def step(slot, done):
+        used = jnp.max(plan_ref[layer, slot]) == kind
+        there = used & (done == 0) if ahead and kind == 1 else used & False
+
+        @pl.when(used & jnp.logical_not(there))
         def _():
             copy(own_ref, slot).wait()
-            real, imag = complex_parts(multiply(full_ref[...], weights[slot]))
-            cosine = jnp.broadcast_to(table_ref[layer, slot, 0][:, :1], (cols, rows))
-            sine = jnp.broadcast_to(table_ref[layer, slot, 1][:, :1], (cols, rows))
-            total_ref[:cols] -= real * cosine - imag * sine
-            total_ref[cols:] -= real * sine + imag * cosine
-
-        return 0
-
-    lax.fori_loop(0, slots, subtract, 0)
+            subtract(slot, weights[slot])
+
+        if ahead and kind == 1:
+            pl.when(there)(lambda: subtract(slot, ahead_ref[...]))
+        return done + used.astype(jnp.int32)
+
+    lax.fori_loop(0, slots, step, jnp.int32(0))
+    if ahead and kind == 2:
+
+        @pl.when(next_found > 0)
+        def _():
+            pltpu.make_async_copy(own_ref.at[layer % layers, 0], ahead_ref, sems.at[slots]).wait()
+
     if out_ref.ndim == 2:
         out_ref[...] = total_ref[...]
     else:
@@ -205,17 +237,20 @@
             transcendentals=0,
         )
 
-    def images(layer, kind, base, blocks):
+    def images(layer, kind, base, blocks, ahead=None):
+        blocks = blocks if ahead is None else [*blocks, ahead]
+        first_weights = pltpu.VMEM(coupling.shape[2:], coupling.dtype)
+        part = jax.ShapeDtypeStruct((wide, rows), jnp.float32)
         return pl.pallas_call(
-            functools.partial(image_kernel, layer, kind, base.ndim == 3),
-            out_shape=copied_shape if kind == 1 else jax.ShapeDtypeStruct((wide, rows), jnp.float32),
+            functools.partial(image_kernel, layer, kind, base.ndim == 3, kind == 2 or ahead is not None),
+            out_shape=copied_shape if kind == 1 else [part, first_weights],
             in_specs=[VMEM] * 2 + [ANY] * 2 + [VMEM] * (1 + len(blocks)),
-            out_specs=VMEM,
+            out_specs=VMEM if kind == 1 else [VMEM] * 2,
             scratch_shapes=[
                 pltpu.VMEM((wide, rows), jnp.float32),
                 full_scratch,
                 pltpu.VMEM((slots, 2, rows, unknowns), jnp.bfloat16),
-                pltpu.SemaphoreType.DMA((slots,)),
+                pltpu.SemaphoreType.DMA((slots + 1,)),
             ],
             compiler_params=params,
             cost_estimate=cost(slots // 2),
@@ -251,8 +286,8 @@
     def run(start, latest, earlier):
         fields = []
         for layer in range(start, deep):
-            base = right if earlier is None else images(layer, 2, right, earlier)
-            copied = images(layer, 1, base, latest)
+            base, ahead = (right, None) if earlier is None else images(layer, 2, right, earlier)
+            copied = images(layer, 1, base, latest, None if ahead is None else held(ahead))
             if layer + 1 < deep:
                 field, next_copied = invert(gather(copied), load(layer, other_inverse, copied), False)
                 fields.append(field)

time: 292 us -> 293 us (level)
    ppermute x2, waiting for transfers between devices: 108 us -> 102 us  [shift(): lax.ppermute(array, ('layer', 'angle'), [(i, i + CORES * peers) for i in...]
    all_to_all x8, waiting for transfers between devices: 45.2 us -> 49.3 us  [gather(): return lax.all_to_all(copied, 'angle', 0, 0)]
  transfers between devices with their start and end apart: 16 -> 16, of which waited for: 11 -> 12; matrix products, arithmetic and copies ran while one was open for 1% -> 2% of each run, Pallas kernels for 9% -> 7%
where the time goes in v1:
time: 293 us
  waiting for transfers between devices  181 us (62%)
  starting transfers between devices  55.8 us (19%)
  Pallas kernels  47 us (16%)
  other arithmetic  5.95 us (2%)
  local copies, waits for them, and re-layouts  3.11 us (1%)
    ppermute x2, waiting for transfers between devices, shift(): lax.ppermute(array, ('layer', 'angle'), [(i, i + CORES * peers) for i in...  102 us
    all_to_all x8, waiting for transfers between devices, gather(): return lax.all_to_all(copied, 'angle', 0, 0)  49.3 us
    all_to_all x8, starting transfers between devices, gather(): return lax.all_to_all(copied, 'angle', 0, 0)  47.4 us
    pallas_call x8, Pallas kernels, images(): pl.pallas_call(functools.partial(image_kernel, layer, kind, base.ndim ==...  33.8 us
    ppermute x5, waiting for transfers between devices, swap(): return lax.ppermute(array, 'layer', pairs)  28.8 us
    pallas_call x4, Pallas kernels, load(): pl.pallas_call(functools.partial(load_kernel, layer), out_shape=pltpu.VME...  6.86 us
  transfers between devices with their start and end apart: 16, of which 12 were waited for; matrix products, arithmetic and copies ran while one was open for 2% of the time, Pallas kernels for 7%

profile of v1, /device:TPU:3, one launch (start us, length us, event | category | flops | bytes accessed | tf_op | source)
XLA Modules:
  0.0 293.0 jit_solution(15329530108571934432)
XLA Ops:
  9.0 27.7 %collective-permute-done.4 = bf16[2,2,256,2048]{3,2,1,0:T(8,128)(2,1)} collective-permute-done((bf16[2,2,256,2048]{3,2,1,0:T(8,128)(2,1)}, bf16[2,2,256,2048]{3,2,1,0:T(8,128)(2,1)}, u32[]{:S(2)}, u32[]{:S(2)}) %collective-permute-start.4) | collective-permute-done | bytes 4194336 | tf_op jit(solution)/shard_map/ppermute | solution.py:38
  39.5 102.4 %collective-permute-done.6 = bf16[96,256]{1,0:T(8,128)(2,1)S(1)} collective-permute-done((bf16[96,256]{1,0:T(8,128)(2,1)S(1)}, bf16[96,256]{1,0:T(8,128)(2,1)S(1)}, u32[]{:S(2)}, u32[]{:S(2)}) %collective-permute-start.6) | collective-permute-done | bytes 49184 | tf_op jit(solution)/shard_map/ppermute | solution.py:44
  141.9 128.3 %conditional.8 = (bf16[96,256]{1,0:T(8,128)(2,1)}, bf16[96,256]{1,0:T(8,128)(2,1)}, bf16[96,256]{1,0:T(8,128)(2,1)}, bf16[8,96,256]{2,1,0:T(8,128)(2,1)}) conditional(s32[]{:T(128)} %convert_element_type.29, () %tuple.43, (f32[5,4,8,128]{3,2,1,0:T(8,128)S(1)}, f32[4,4,2,48,128]{4,3,2,1,0:T(8,128)S(1)}, bf16[2,4,2,256,2048]{4,3,2,1,0:T(8,128)(2,1)}, ...), branch_computations={%region_6.7_spmd, %region_7.8_spmd} | conditional | flops 3825205248 | bytes 64618808 | solution.py:301
  142.8 5.7 %all-to-all-start.7 = ((bf16[8,96,256]{2,1,0:T(8,128)(2,1)}), bf16[8,96,256]{2,1,0:T(8,128)(2,1)S(1)}, u32[]{:S(2)}, u32[]{:S(2)}) async-start(bf16[8,96,256]{2,1,0:T(8,128)(2,1)} %copies.3), calls=%async_computation.7 | async-start | bytes 786432 | tf_op jit(solution)/shard_map/cond/branch_1_fun/all_to_all | solution.py:48
  151.4 5.2 %all-to-all-done.7.refs_0_ = bf16[8,96,256]{2,1,0:T(8,128)(2,1)S(1)} async-done(((bf16[8,96,256]{2,1,0:T(8,128)(2,1)}), bf16[8,96,256]{2,1,0:T(8,128)(2,1)S(1)}, u32[]{:S(2)}, u32[]{:S(2)}) %all-to-all-start.7) | async-done | bytes 393248 | tf_op jit(solution)/shard_map/cond/branch_1_fun/all_to_all | solution.py:48
  160.2 6.4 %all-to-all-start.8 = ((bf16[8,96,256]{2,1,0:T(8,128)(2,1)}), bf16[8,96,256]{2,1,0:T(8,128)(2,1)S(1)}, u32[]{:S(2)}, u32[]{:S(2)}) async-start(bf16[8,96,256]{2,1,0:T(8,128)(2,1)} %images_1.10._), calls=%async_computation.8 | async-start | bytes 786432 | tf_op jit(solution)/shard_map/cond/branch_1_fun/all_to_all | solution.py:48
  168.3 6.6 %all-to-all-done.8.blocks_ref = bf16[8,96,256]{2,1,0:T(8,128)(2,1)S(1)} async-done(((bf16[8,96,256]{2,1,0:T(8,128)(2,1)}), bf16[8,96,256]{2,1,0:T(8,128)(2,1)S(1)}, u32[]{:S(2)}, u32[]{:S(2)}) %all-to-all-start.8) | async-done | bytes 393248 | tf_op jit(solution)/shard_map/cond/branch_1_fun/all_to_all | solution.py:48
  176.5 6.5 %all-to-all-start.9 = ((bf16[8,96,256]{2,1,0:T(8,128)(2,1)}), bf16[8,96,256]{2,1,0:T(8,128)(2,1)S(1)}, u32[]{:S(2)}, u32[]{:S(2)}) async-start(bf16[8,96,256]{2,1,0:T(8,128)(2,1)} %get-tuple-element.113), calls=%async_computation.9 | async-start | bytes 786432 | tf_op jit(solution)/shard_map/cond/branch_1_fun/all_to_all | solution.py:48
  182.9 4.9 %images_2.9 = (f32[96,256]{1,0:T(8,128)S(1)}, bf16[2,256,2048]{2,1,0:T(8,128)(2,1)S(1)}) custom-call(f32[5,4,8,128]{3,2,1,0:T(8,128)S(1)} %get-tuple-element.100.plan_ref, f32[4,4,2,48,128]{4,3,2,1,0:T(8,128)} %copy-done.3, bf16[2,4,2,256,2048]{4,3,2,1,0:T(8,128)(2,1)} %get-tuple-element.104.own_ref, ...), custom_call_target="tpu_custom_call" | custom-call | flops 402653184 | bytes 4194304 | tf_op jit(solution)/shard_map/cond/branch_1_fun/images_2/pallas_call | solution.py:244
  187.8 4.2 %all-to-all-done.9.refs_0_ = bf16[8,96,256]{2,1,0:T(8,128)(2,1)S(1)} async-done(((bf16[8,96,256]{2,1,0:T(8,128)(2,1)}), bf16[8,96,256]{2,1,0:T(8,128)(2,1)S(1)}, u32[]{:S(2)}, u32[]{:S(2)}) %all-to-all-start.9) | async-done | bytes 393248 | tf_op jit(solution)/shard_map/cond/branch_1_fun/all_to_all | solution.py:48
  192.0 4.5 %images_1.11._ = bf16[8,96,256]{2,1,0:T(8,128)(2,1)} custom-call(f32[5,4,8,128]{3,2,1,0:T(8,128)S(1)} %get-tuple-element.100.plan_ref, f32[4,4,2,48,128]{4,3,2,1,0:T(8,128)} %copy-done.3, bf16[2,4,2,256,2048]{4,3,2,1,0:T(8,128)(2,1)} %get-tuple-element.104.own_ref, bf16[2,4,2,256,2048]{4,3,2,1,0:T(8,128)(2,1)} %get-tuple-element.105.other_ref, ...), custom_call_target="tpu_custom_call" | custom-call | flops 402653184 | bytes 4194304 | tf_op jit(solution)/shard_map/cond/branch_1_fun/images_1/pallas_call | solution.py:244
  196.5 5.7 %all-to-all-start.10 = ((bf16[8,96,256]{2,1,0:T(8,128)(2,1)}), bf16[8,96,256]{2,1,0:T(8,128)(2,1)S(1)}, u32[]{:S(2)}, u32[]{:S(2)}) async-start(bf16[8,96,256]{2,1,0:T(8,128)(2,1)} %images_1.11._), calls=%async_computation.10 | async-start | bytes 786432 | tf_op jit(solution)/shard_map/cond/branch_1_fun/all_to_all | solution.py:48
  204.0 7.3 %all-to-all-done.10.blocks_ref = bf16[8,96,256]{2,1,0:T(8,128)(2,1)S(1)} async-done(((bf16[8,96,256]{2,1,0:T(8,128)(2,1)}), bf16[8,96,256]{2,1,0:T(8,128)(2,1)S(1)}, u32[]{:S(2)}, u32[]{:S(2)}) %all-to-all-start.10) | async-done | bytes 393248 | tf_op jit(solution)/shard_map/cond/branch_1_fun/all_to_all | solution.py:48
  212.9 5.7 %all-to-all-start.11 = ((bf16[8,96,256]{2,1,0:T(8,128)(2,1)}), bf16[8,96,256]{2,1,0:T(8,128)(2,1)S(1)}, u32[]{:S(2)}, u32[]{:S(2)}) async-start(bf16[8,96,256]{2,1,0:T(8,128)(2,1)} %get-tuple-element.117), calls=%async_computation.11 | async-start | bytes 786432 | tf_op jit(solution)/shard_map/cond/branch_1_fun/all_to_all | solution.py:48
  221.6 6.1 %all-to-all-done.11.refs_0_ = bf16[8,96,256]{2,1,0:T(8,128)(2,1)S(1)} async-done(((bf16[8,96,256]{2,1,0:T(8,128)(2,1)}), bf16[8,96,256]{2,1,0:T(8,128)(2,1)S(1)}, u32[]{:S(2)}, u32[]{:S(2)}) %all-to-all-start.11) | async-done | bytes 393248 | tf_op jit(solution)/shard_map/cond/branch_1_fun/all_to_all | solution.py:48
  227.7 5.5 %images_1.12._ = bf16[8,96,256]{2,1,0:T(8,128)(2,1)} custom-call(f32[5,4,8,128]{3,2,1,0:T(8,128)S(1)} %get-tuple-element.100.plan_ref, f32[4,4,2,48,128]{4,3,2,1,0:T(8,128)} %copy-done.3, bf16[2,4,2,256,2048]{4,3,2,1,0:T(8,128)(2,1)} %get-tuple-element.104.own_ref, bf16[2,4,2,256,2048]{4,3,2,1,0:T(8,128)(2,1)} %get-tuple-element.105.other_ref, ...), custom_call_target="tpu_custom_call" | custom-call | flops 402653184 | bytes 4194304 | tf_op jit(solution)/shard_map/cond/branch_1_fun/images_1/pallas_call | solution.py:244
  233.2 5.7 %all-to-all-start.12 = ((bf16[8,96,256]{2,1,0:T(8,128)(2,1)}), bf16[8,96,256]{2,1,0:T(8,128)(2,1)S(1)}, u32[]{:S(2)}, u32[]{:S(2)}) async-start(bf16[8,96,256]{2,1,0:T(8,128)(2,1)} %images_1.12._), calls=%async_computation.12 | async-start | bytes 786432 | tf_op jit(solution)/shard_map/cond/branch_1_fun/all_to_all | solution.py:48
  240.7 7.3 %all-to-all-done.12.blocks_ref = bf16[8,96,256]{2,1,0:T(8,128)(2,1)S(1)} async-done(((bf16[8,96,256]{2,1,0:T(8,128)(2,1)}), bf16[8,96,256]{2,1,0:T(8,128)(2,1)S(1)}, u32[]{:S(2)}, u32[]{:S(2)}) %all-to-all-start.12) | async-done | bytes 393248 | tf_op jit(solution)/shard_map/cond/branch_1_fun/all_to_all | solution.py:48
  249.6 5.7 %all-to-all-start.13 = ((bf16[8,96,256]{2,1,0:T(8,128)(2,1)}), bf16[8,96,256]{2,1,0:T(8,128)(2,1)S(1)}, u32[]{:S(2)}, u32[]{:S(2)}) async-start(bf16[8,96,256]{2,1,0:T(8,128)(2,1)} %get-tuple-element.121), calls=%async_computation.13 | async-start | bytes 786432 | tf_op jit(solution)/shard_map/cond/branch_1_fun/all_to_all | solution.py:48
  259.2 5.2 %all-to-all-done.13.refs_0_ = bf16[8,96,256]{2,1,0:T(8,128)(2,1)S(1)} async-done(((bf16[8,96,256]{2,1,0:T(8,128)(2,1)}), bf16[8,96,256]{2,1,0:T(8,128)(2,1)S(1)}, u32[]{:S(2)}, u32[]{:S(2)}) %all-to-all-start.13) | async-done | bytes 393248 | tf_op jit(solution)/shard_map/cond/branch_1_fun/all_to_all | solution.py:48
  264.4 5.5 %images_1.13 = bf16[8,96,256]{2,1,0:T(8,128)(2,1)} custom-call(f32[5,4,8,128]{3,2,1,0:T(8,128)S(1)} %get-tuple-element.100.plan_ref, f32[4,4,2,48,128]{4,3,2,1,0:T(8,128)} %copy-done.3, bf16[2,4,2,256,2048]{4,3,2,1,0:T(8,128)(2,1)} %get-tuple-element.104.own_ref, bf16[2,4,2,256,2048]{4,3,2,1,0:T(8,128)(2,1)} %get-tuple-element.105.other_ref, ...), custom_call_target="tpu_custom_call" | custom-call | flops 402653184 | bytes 4194304 | tf_op jit(solution)/shard_map/cond/branch_1_fun/images_1/pallas_call | solution.py:244
  270.2 15.7 %conditional.9 = (bf16[96,256]{1,0:T(8,128)(2,1)S(1)}) conditional(s32[]{:T(128)} %convert_element_type.29, () %tuple.53, (f32[5,4,8,128]{3,2,1,0:T(8,128)S(1)}, bf16[2,2,256,2048]{3,2,1,0:T(8,128)(2,1)}, bf16[2,2,256,2048]{3,2,1,0:T(8,128)(2,1)}, bf16[8,96,256]{2,1,0:T(8,128)(2,1)}) %tuple.54), branch_computations={%region_8.9_spmd, %region_9.10_spmd} | conditional | flops 201326592 | bytes 7471144 | solution.py:301
  270.2 5.9 %all-to-all-start.14 = ((bf16[8,96,256]{2,1,0:T(8,128)(2,1)}), bf16[8,96,256]{2,1,0:T(8,128)(2,1)S(1)}, u32[]{:S(2)}, u32[]{:S(2)}) async-start(bf16[8,96,256]{2,1,0:T(8,128)(2,1)} %get-tuple-element.126._), calls=%async_computation.14 | async-start | bytes 786432 | tf_op jit(solution)/shard_map/cond/branch_1_fun/all_to_all | solution.py:48
  277.8 7.3 %all-to-all-done.14.blocks_ref = bf16[8,96,256]{2,1,0:T(8,128)(2,1)S(1)} async-done(((bf16[8,96,256]{2,1,0:T(8,128)(2,1)}), bf16[8,96,256]{2,1,0:T(8,128)(2,1)S(1)}, u32[]{:S(2)}, u32[]{:S(2)}) %all-to-all-start.14) | async-done | bytes 393248 | tf_op jit(solution)/shard_map/cond/branch_1_fun/all_to_all | solution.py:48
  (78 shorter events, 45.2 us)
Async XLA Ops:
  1.0 4.1 %collective-permute-start = (bf16[2,96,256]{2,1,0:T(8,128)(2,1)S(1)}, bf16[2,96,256]{2,1,0:T(8,128)(2,1)S(1)}, u32[]{:S(2)}, u32[]{:S(2)}) collective-permute-start(bf16[2,96,256]{2,1,0:T(8,128)(2,1)S(1)} %bitcast.59), channel_id=1, source_target_pairs={{0,8},{8,0},{16,24},{24,16},{1,9},{9,1},{17,25},{25,17},{2,10},{10... | collective-permute-start | bytes 294920 | tf_op jit(solution)/shard_map/ppermute | solution.py:38
  3.1 1.2 collective-permute-start.1
  5.1 31.6 %copy-start.4 = (bf16[4,96,256]{2,1,0:T(8,128)(2,1)}, bf16[4,96,256]{2,1,0:T(8,128)(2,1)S(1)}, u32[]{:S(2)}) copy-start(bf16[4,96,256]{2,1,0:T(8,128)(2,1)S(1)} %maximum_select_fusion) | copy-start | bytes 589828
  5.1 31.6 %collective-permute-start.2 = (bf16[2,4,2,256,2048]{4,3,2,1,0:T(8,128)(2,1)}, bf16[2,4,2,256,2048]{4,3,2,1,0:T(8,128)(2,1)}, u32[]{:S(2)}, u32[]{:S(2)}) collective-permute-start(bf16[2,4,2,256,2048]{4,3,2,1,0:T(8,128)(2,1)} %param.18), channel_id=1, source_target_pairs={{0,8},{8,0},{16,24},{24,16},{1,9},{9,1},{17,25},{25,17},{2,10},{10... | collective-permute-start | bytes 50331656 | tf_op jit(solution)/shard_map/ppermute | solution.py:38
  5.4 31.2 %collective-permute-start.4 = (bf16[2,2,256,2048]{3,2,1,0:T(8,128)(2,1)}, bf16[2,2,256,2048]{3,2,1,0:T(8,128)(2,1)}, u32[]{:S(2)}, u32[]{:S(2)}) collective-permute-start(bf16[2,2,256,2048]{3,2,1,0:T(8,128)(2,1)} %param.17), channel_id=1, source_target_pairs={{0,8},{8,0},{16,24},{24,16},{1,9},{9,1},{17,25},{25,17},{2,10},{10... | collective-permute-start | bytes 12582920 | tf_op jit(solution)/shard_map/ppermute | solution.py:38
  8.3 0.7 collective-permute-start.3
  36.7 105.2 %collective-permute-start.5 = (bf16[8,96,256]{2,1,0:T(8,128)(2,1)}, bf16[8,96,256]{2,1,0:T(8,128)(2,1)}, u32[]{:S(2)}, u32[]{:S(2)}) collective-permute-start(bf16[8,96,256]{2,1,0:T(8,128)(2,1)} %get-tuple-element.151), channel_id=1, source_target_pairs={{0,16},{1,17},{2,18},{3,19},{4,20},{5,21},{6,22},{7,23},{8,24},{9,... | collective-permute-start | bytes 1179656 | tf_op jit(solution)/shard_map/ppermute | solution.py:44
  38.0 103.9 %copy-start = (f32[4,4,2,48,128]{4,3,2,1,0:T(8,128)S(1)}, f32[4,4,2,48,128]{4,3,2,1,0:T(8,128)}, u32[]{:S(2)}) copy-start(f32[4,4,2,48,128]{4,3,2,1,0:T(8,128)} %broadcast_in_dim.10) | copy-start | bytes 2359300
  38.0 103.8 %copy-start.10 = (bf16[96,256]{1,0:T(8,128)(2,1)}, bf16[96,256]{1,0:T(8,128)(2,1)S(1)}, u32[]{:S(2)}) copy-start(bf16[96,256]{1,0:T(8,128)(2,1)S(1)} %get-tuple-element.193) | copy-start | bytes 147460
  38.0 103.8 %collective-permute-start.6 = (bf16[96,256]{1,0:T(8,128)(2,1)S(1)}, bf16[96,256]{1,0:T(8,128)(2,1)S(1)}, u32[]{:S(2)}, u32[]{:S(2)}) collective-permute-start(bf16[96,256]{1,0:T(8,128)(2,1)S(1)} %get-tuple-element.193), channel_id=1, source_target_pairs={{0,16},{1,17},{2,18},{3,19},{4,20},{5,21},{6,22},{7,23},{8,24},{9,... | collective-permute-start | bytes 147464 | tf_op jit(solution)/shard_map/ppermute | solution.py:44
  142.8 13.8 %all-to-all-start.7 = ((bf16[8,96,256]{2,1,0:T(8,128)(2,1)}), bf16[8,96,256]{2,1,0:T(8,128)(2,1)S(1)}, u32[]{:S(2)}, u32[]{:S(2)}) async-start(bf16[8,96,256]{2,1,0:T(8,128)(2,1)} %copies.3), calls=%async_computation.7 | async-start | bytes 786432 | tf_op jit(solution)/shard_map/cond/branch_1_fun/all_to_all | solution.py:48
  160.2 14.7 %all-to-all-start.8 = ((bf16[8,96,256]{2,1,0:T(8,128)(2,1)}), bf16[8,96,256]{2,1,0:T(8,128)(2,1)S(1)}, u32[]{:S(2)}, u32[]{:S(2)}) async-start(bf16[8,96,256]{2,1,0:T(8,128)(2,1)} %images_1.10._), calls=%async_computation.8 | async-start | bytes 786432 | tf_op jit(solution)/shard_map/cond/branch_1_fun/all_to_all | solution.py:48
  176.5 15.5 %all-to-all-start.9 = ((bf16[8,96,256]{2,1,0:T(8,128)(2,1)}), bf16[8,96,256]{2,1,0:T(8,128)(2,1)S(1)}, u32[]{:S(2)}, u32[]{:S(2)}) async-start(bf16[8,96,256]{2,1,0:T(8,128)(2,1)} %get-tuple-element.113), calls=%async_computation.9 | async-start | bytes 786432 | tf_op jit(solution)/shard_map/cond/branch_1_fun/all_to_all | solution.py:48
  196.5 14.8 %all-to-all-start.10 = ((bf16[8,96,256]{2,1,0:T(8,128)(2,1)}), bf16[8,96,256]{2,1,0:T(8,128)(2,1)S(1)}, u32[]{:S(2)}, u32[]{:S(2)}) async-start(bf16[8,96,256]{2,1,0:T(8,128)(2,1)} %images_1.11._), calls=%async_computation.10 | async-start | bytes 786432 | tf_op jit(solution)/shard_map/cond/branch_1_fun/all_to_all | solution.py:48
  212.9 14.8 %all-to-all-start.11 = ((bf16[8,96,256]{2,1,0:T(8,128)(2,1)}), bf16[8,96,256]{2,1,0:T(8,128)(2,1)S(1)}, u32[]{:S(2)}, u32[]{:S(2)}) async-start(bf16[8,96,256]{2,1,0:T(8,128)(2,1)} %get-tuple-element.117), calls=%async_computation.11 | async-start | bytes 786432 | tf_op jit(solution)/shard_map/cond/branch_1_fun/all_to_all | solution.py:48
  233.2 14.8 %all-to-all-start.12 = ((bf16[8,96,256]{2,1,0:T(8,128)(2,1)}), bf16[8,96,256]{2,1,0:T(8,128)(2,1)S(1)}, u32[]{:S(2)}, u32[]{:S(2)}) async-start(bf16[8,96,256]{2,1,0:T(8,128)(2,1)} %images_1.12._), calls=%async_computation.12 | async-start | bytes 786432 | tf_op jit(solution)/shard_map/cond/branch_1_fun/all_to_all | solution.py:48
  249.6 14.8 %all-to-all-start.13 = ((bf16[8,96,256]{2,1,0:T(8,128)(2,1)}), bf16[8,96,256]{2,1,0:T(8,128)(2,1)S(1)}, u32[]{:S(2)}, u32[]{:S(2)}) async-start(bf16[8,96,256]{2,1,0:T(8,128)(2,1)} %get-tuple-element.121), calls=%async_computation.13 | async-start | bytes 786432 | tf_op jit(solution)/shard_map/cond/branch_1_fun/all_to_all | solution.py:48
  270.2 15.8 %copy-start.11 = (bf16[96,256]{1,0:T(8,128)(2,1)S(1)}, bf16[96,256]{1,0:T(8,128)(2,1)}, u32[]{:S(2)}) copy-start(bf16[96,256]{1,0:T(8,128)(2,1)} %copy-done.10) | copy-start | bytes 147460
  270.2 15.8 %copy-start.13 = (bf16[96,256]{1,0:T(8,128)(2,1)S(1)}, bf16[96,256]{1,0:T(8,128)(2,1)}, u32[]{:S(2)}) copy-start(bf16[96,256]{1,0:T(8,128)(2,1)} %get-tuple-element.158) | copy-start | bytes 147460
  270.2 16.6 %copy-start.12 = (bf16[96,256]{1,0:T(8,128)(2,1)S(1)}, bf16[96,256]{1,0:T(8,128)(2,1)}, u32[]{:S(2)}) copy-start(bf16[96,256]{1,0:T(8,128)(2,1)} %get-tuple-element.156) | copy-start | bytes 147460
  270.2 16.6 %copy-start.14 = (bf16[96,256]{1,0:T(8,128)(2,1)S(1)}, bf16[96,256]{1,0:T(8,128)(2,1)}, u32[]{:S(2)}) copy-start(bf16[96,256]{1,0:T(8,128)(2,1)} %get-tuple-element.154) | copy-start | bytes 147460
  270.2 22.1 %copy-start.15 = (bf16[96,256]{1,0:T(8,128)(2,1)S(1)}, bf16[96,256]{1,0:T(8,128)(2,1)}, u32[]{:S(2)}) copy-start(bf16[96,256]{1,0:T(8,128)(2,1)} %get-tuple-element.160) | copy-start | bytes 147460
  270.2 14.9 %all-to-all-start.14 = ((bf16[8,96,256]{2,1,0:T(8,128)(2,1)}), bf16[8,96,256]{2,1,0:T(8,128)(2,1)S(1)}, u32[]{:S(2)}, u32[]{:S(2)}) async-start(bf16[8,96,256]{2,1,0:T(8,128)(2,1)} %get-tuple-element.126._), calls=%async_computation.14 | async-start | bytes 786432 | tf_op jit(solution)/shard_map/cond/branch_1_fun/all_to_all | solution.py:48
  287.7 4.6 %collective-permute-start.7 = (bf16[2,96,256]{2,1,0:T(8,128)(2,1)S(1)}, bf16[2,96,256]{2,1,0:T(8,128)(2,1)S(1)}, u32[]{:S(2)}, u32[]{:S(2)}) collective-permute-start(bf16[2,96,256]{2,1,0:T(8,128)(2,1)S(1)} %maximum_select_fusion.3), channel_id=1, source_target_pairs={{0,8},{8,0},{16,24},{24,16},{1,9},{9,1},{17,25},{25,17},{2,10},{10... | collective-permute-start | bytes 294920 | tf_op jit(solution)/shard_map/ppermute | solution.py:38
  (4 other events, 31.5 us)
